TPU v7x, 32 devices: a whole 2x2x4 slice. The times are simulated.
32 devices in a mesh: groups: 2 (over y), field: 4 (over x, core), wave: 4 (over z).
Axes of the slice: x: 2, y: 2, z: 4, core: 2. Of those that a mesh axis runs over, the one named last changes fastest.
Arguments:
- mode_basis: bfloat16 [22, 512, 512], P(None, 'wave'), may hold values from -6 to 6
- coef_table: bfloat16 [4096, 22], replicated, may hold values from -1.5 to 1.5
- table_index: int32 [64], P(('groups', 'field')), parts along dimension 0, may hold values from 0 to 4095
- wave_lengths: float32 [8], P('wave'), may hold values from 0.32 to 1.05
- sed_table: float32 [1024, 8], replicated, may hold values from 0.05 to 1
- template_ids: int32 [64, 8], P(('groups', 'field')), parts along dimension 0, may hold values from 0 to 1023
Outputs:
- mixed: bfloat16 [64, 8, 256, 256], P(('groups', 'field'), None, 'wave'), parts along dimension 0
There are 2 independent parts, one for each index of `groups`. A program takes and returns all parts, laid end to end along the dimension named above; an argument that names none is the same for every part. Nothing has to cross between parts.
All inputs are finite; a program needn't handle non-finite values.
Results may differ from a plain program's by a relative error of at most 0.0065.
Values may be sent and summed in bfloat16 or wider, within the bound.
A program may use at most 128 MiB of HBM per device.

v0:
```python
import math
import jax
import jax.numpy as jnp
from jax import lax
from jax.sharding import PartitionSpec as P

PUP = 512
PIX = 256
TWO_PI = 2.0 * math.pi
SAMPLING = 0.25
EPSILON = 1e-06


def transform_table(wave_lengths, pixels, pupil_side):
    pixel_offset = jnp.arange(pixels, dtype=jnp.int32) - pixels // 2
    pupil_offset = 2 * jnp.arange(pupil_side, dtype=jnp.int32) - pupil_side + 1
    products = (pixel_offset[:, None] * pupil_offset[None, :]).astype(jnp.float32)
    factor = TWO_PI * SAMPLING / (2.0 * pupil_side) / wave_lengths
    angles = products[None, :, :] * factor[:, None, None]
    cosine = jnp.cos(angles)
    sine_part = jnp.sin(angles)
    upper_half = jnp.concatenate([cosine, sine_part], axis=2)
    lower_half = jnp.concatenate([-sine_part, cosine], axis=2)
    return jnp.concatenate([upper_half, lower_half], axis=1).astype(jnp.bfloat16)


def aperture_rows(row_start, row_count, pupil_side):
    row_pos = 2 * (row_start + jnp.arange(row_count, dtype=jnp.int32)) - pupil_side + 1
    col_pos = 2 * jnp.arange(pupil_side, dtype=jnp.int32) - pupil_side + 1
    radius_sq = row_pos[:, None] * row_pos[:, None] + col_pos[None, :] * col_pos[None, :]
    inner_edge = 61 * pupil_side // 100
    inside = (radius_sq <= pupil_side * pupil_side) & (radius_sq >= inner_edge * inner_edge)
    return inside.astype(jnp.float32)


def pupil_section(path_rows, wave_lengths, kernel_table, row_start):
    row_count = path_rows.shape[1]
    pupil_side = path_rows.shape[2]
    opening = aperture_rows(row_start, row_count, pupil_side)
    phase_map = path_rows[:, None, :, :] * (TWO_PI / wave_lengths)[None, :, None, None]
    field_real = opening * jnp.cos(phase_map)
    field_imag = opening * jnp.sin(phase_map)
    pupil_field = jnp.concatenate([field_real, field_imag], axis=3).astype(jnp.bfloat16)
    first_pass = jnp.einsum(
        "flxy,luy->flxu", pupil_field, kernel_table, preferred_element_type=jnp.float32
    )
    return first_pass.astype(jnp.bfloat16)


def finish_section(first_pass, kernel_table):
    pixels = first_pass.shape[3] // 2
    stacked = jnp.concatenate([first_pass[..., :pixels], first_pass[..., pixels:]], axis=2)
    image_field = jnp.einsum(
        "lux,flxv->fluv", kernel_table, stacked, preferred_element_type=jnp.float32
    )
    intensity = (
        image_field[:, :, :pixels] * image_field[:, :, :pixels]
        + image_field[:, :, pixels:] * image_field[:, :, pixels:]
    )
    mean_level = jnp.mean(intensity, axis=(2, 3), keepdims=True)
    return (intensity / (mean_level + EPSILON)).astype(jnp.bfloat16)


def local(mode_basis, coef_table, table_index, wave_lengths, sed_table, template_ids):
    kernel_table = transform_table(wave_lengths, PIX, PUP)
    table_rows = coef_table.shape[0]
    selector = (table_index[:, None] == jnp.arange(table_rows, dtype=jnp.int32)[None, :]).astype(
        jnp.bfloat16
    )
    coeffs = jnp.dot(selector, coef_table, preferred_element_type=jnp.float32).astype(jnp.bfloat16)
    mode_count = mode_basis.shape[0]
    positions = coeffs.shape[0]
    whole_basis = lax.all_gather(mode_basis, "wave", axis=1, tiled=True)
    path_diff = jnp.dot(
        coeffs, whole_basis.reshape(mode_count, -1), preferred_element_type=jnp.float32
    )
    path_diff = path_diff.reshape(positions, PUP, PUP)
    first_pass = pupil_section(path_diff, wave_lengths, kernel_table, 0)
    spectra = finish_section(first_pass, kernel_table)
    pixel_slabs = lax.all_to_all(spectra, "wave", split_axis=2, concat_axis=1, tiled=True)
    sed_rows = sed_table.shape[0]
    one_hot = (
        template_ids[:, :, None] == jnp.arange(sed_rows, dtype=jnp.int32)[None, None, :]
    ).astype(jnp.float32)
    raw_weights = jnp.einsum("fjn,nl->fjl", one_hot, sed_table, precision=lax.Precision.HIGHEST)
    weights = (raw_weights / jnp.sum(raw_weights, axis=2, keepdims=True)).astype(jnp.bfloat16)
    mixed = jnp.einsum("fjl,flrp->fjrp", weights, pixel_slabs, preferred_element_type=jnp.float32)
    return mixed.astype(jnp.bfloat16)


def solution(mesh):
    return jax.shard_map(
        local,
        mesh=mesh,
        in_specs=(
            P(None, "wave", None),
            P(),
            P(("groups", "field")),
            P("wave"),
            P(),
            P(("groups", "field"), None),
        ),
        out_specs=P(("groups", "field"), None, "wave", None),
        check_vma=False,
    )
```

profile of v0, /device:TPU:0, one launch (start us, length us, event | category | flops | bytes accessed | tf_op | source)
XLA Modules:
  0.0 431.0 jit_solution(3552195632405545953)
XLA Ops:
  6.5 0.0 copy-start
  6.5 0.0 all-gather.2.cloned.1.call-start
  6.5 0.7 all-gather.2.cloned.1.call-update
  7.3 0.7 broadcast_divide_fusion.1
  8.0 0.1 multiply_convert_fusion
  8.1 0.2 fusion.30
  8.3 4.1 fusion.22
  12.4 0.0 copy-start.3
  12.4 200.3 %all-gather.2.cloned.1.call-done = bf16[22,512,512]{2,1,0:T(8,128)(2,1)} async-done(((bf16[22,128,512]{2,1,0:T(8,128)(2,1)}), bf16[22,512,512]{2,1,0:T(8,128)(2,1)}) %all-gather.2.cloned.1.call-update) | async-done | bytes 11534352 | tf_op jit(solution)/shard_map/all_gather | solution.py:73
  212.7 10.0 %slice_bitcast_fusion = bf16[512,512,22]{1,0,2:T(8,128)(2,1)} fusion(bf16[22,512,512]{2,1,0:T(8,128)(2,1)} %all-gather.2.cloned.1.call-done), kind=kLoop, calls=%fused_computation.13 | loop fusion | bytes 23068672 | tf_op jit(solution)/shard_map/reshape.39
  222.7 0.0 copy-done
  222.7 0.0 copy-done.3
  222.7 24.2 %fusion.9 = f32[8,512,512]{2,0,1:T(8,128)} fusion(bf16[512,512,22]{1,0,2:T(8,128)(2,1)} %slice_bitcast_fusion, bf16[4096,22]{0,1:T(8,128)(2,1)S(1)} %copy-done, s32[8]{0:T(128)S(1)} %copy-done.3), kind=kOutput, calls=%fused_computation.11 | convolution fusion | flops 93749424 | bytes 20103200 | tf_op jit(solution)/shard_map/dot_general | solution.py:74
  247.0 8.2 %copy.20 = f32[8,512,512]{2,1,0:T(8,128)S(1)} copy(f32[8,512,512]{2,0,1:T(8,128)} %fusion.9) | data formatting | bytes 16777216 | tf_op jit(solution)/shard_map/dot_general | solution.py:74
  255.2 64.3 %fusion.2 = (bf16[8,2,512,512]{3,2,0,1:T(8,128)(2,1)}, bf16[8,2,512,512]{3,2,0,1:T(8,128)(2,1)}) fusion(f32[2]{0:T(128)S(1)} %get-tuple-element.13, f32[8,512,512]{2,1,0:T(8,128)S(1)} %copy.20, f32[512,512]{1,0:T(8,128)S(1)} %fusion.30), kind=kLoop, calls=%fused_computation.4 | loop fusion | flops 20971520 | bytes 26214408 | tf_op jit(solution)/shard_map/convert
  319.5 14.6 %convert_bitcast_fusion = bf16[8,2,512,512]{3,2,0,1:T(8,128)(2,1)} fusion(bf16[8,2,512,512]{3,2,0,1:T(8,128)(2,1)} %get-tuple-element.6, bf16[8,2,512,512]{3,2,0,1:T(8,128)(2,1)} %get-tuple-element.5, bf16[2,256,512]{2,1,0:T(8,128)(2,1)S(1)} %get-tuple-element.11, bf16[2,256,512]{2,1,0:T(8,128)(2,1)S(1)} %get-tuple-element.10, ...), kind=kOutput, calls=%fused_computation.18 | convolution fusion | flops 8636071936 | bytes 26738688 | tf_op jit(solution)/shard_map/flxy,luy->flxu/dot_general | solution.py:44
  334.1 5.8 %fusion.41 = (bf16[8,2,512,256]{3,2,0,1:T(8,128)(2,1)}, bf16[8,2,512,256]{3,2,0,1:T(8,128)(2,1)}) fusion(bf16[8,2,512,512]{3,2,0,1:T(8,128)(2,1)} %convert_bitcast_fusion), kind=kLoop, calls=%fused_computation.58 | loop fusion | bytes 16777216 | tf_op jit(solution)/shard_map/slice | solution.py:52
  339.9 11.0 %fusion.18 = f32[8,2,512,256]{2,3,0,1:T(8,128)} fusion(bf16[8,2,512,256]{3,2,0,1:T(8,128)(2,1)} %get-tuple-element.8, bf16[8,2,512,256]{3,2,0,1:T(8,128)(2,1)} %get-tuple-element.7, bf16[2,256,512]{2,1,0:T(8,128)(2,1)S(1)} %get-tuple-element.11, bf16[2,256,512]{2,1,0:T(8,128)(2,1)S(1)} %get-tuple-element.10, bf16[2,256,512]{2,1,0:T(8,128)(2,1)S(1)} %get-tuple-element.9), kind=kOutput, calls=%fused_computation.23 | convolution fusion | flops 4320133120 | bytes 18350080 | tf_op jit(solution)/shard_map/lux,flxv->fluv/dot_general | solution.py:53
  351.0 4.3 fusion.31
  355.3 1.6 copy-done.2
  356.8 0.8 divide_convert_fusion
  357.6 0.0 copy-start.4
  357.6 0.0 copy-start.5
  357.6 3.1 copy.22
  360.7 3.6 all-to-all-start
  364.3 0.0 copy-done.4
  364.3 1.0 fusion.32
  365.4 47.6 %all-to-all-done = bf16[8,2,256,256]{3,0,1,2:T(8,128)(2,1)S(1)} async-done(((bf16[8,2,256,256]{3,0,1,2:T(8,128)(2,1)}), bf16[8,2,256,256]{3,0,1,2:T(8,128)(2,1)S(1)}, u32[]{:S(2)}, u32[]{:S(2)}) %all-to-all-start) | async-done | bytes 2097184 | tf_op jit(solution)/shard_map/all_to_all | solution.py:80
  413.0 2.9 copy.24
  415.9 2.8 all_to_all.16
  418.7 2.0 convolution_convert_fusion
  420.7 3.5 copy.26
  (8 shorter events, 0.0 us)
Async XLA Ops:
  6.5 216.2 %copy-start = (bf16[4096,22]{0,1:T(8,128)(2,1)S(1)}, bf16[4096,22]{0,1:T(8,128)(2,1)}, u32[]{:S(2)}) copy-start(bf16[4096,22]{0,1:T(8,128)(2,1)} %param.7) | copy-start | bytes 540676
  6.5 206.2 %all-gather.2.cloned.1.call-start = ((), (), s32[]{:S(2)}) async-start(), calls=%async_computation.1 | async-start | bytes 14417920 | tf_op jit(solution)/shard_map/all_gather | solution.py:73
  12.4 210.3 %copy-start.3 = (s32[8]{0:T(128)S(1)}, s32[8]{0:T(128)}, u32[]{:S(2)}) copy-start(s32[8]{0:T(128)} %param.8) | copy-start | bytes 100
  351.0 5.8 %copy-start.2 = (f32[8,2,512,256]{2,3,0,1:T(8,128)S(1)}, f32[8,2,512,256]{2,3,0,1:T(8,128)}, u32[]{:S(2)}) copy-start(f32[8,2,512,256]{2,3,0,1:T(8,128)} %fusion.18) | copy-start | bytes 25165828
  357.6 6.7 %copy-start.4 = (f32[1024,8]{0,1:T(8,128)S(1)}, f32[1024,8]{0,1:T(8,128)}, u32[]{:S(2)}) copy-start(f32[1024,8]{0,1:T(8,128)} %param.10) | copy-start | bytes 98308
  357.6 6.7 %copy-start.5 = (s32[8,8]{1,0:T(8,128)S(1)}, s32[8,8]{1,0:T(8,128)}, u32[]{:S(2)}) copy-start(s32[8,8]{1,0:T(8,128)} %param.11) | copy-start | bytes 772
  360.7 52.3 %all-to-all-start = ((bf16[8,2,256,256]{3,0,1,2:T(8,128)(2,1)}), bf16[8,2,256,256]{3,0,1,2:T(8,128)(2,1)S(1)}, u32[]{:S(2)}, u32[]{:S(2)}) async-start(bf16[8,2,256,256]{3,0,1,2:T(8,128)(2,1)} %copy.22), calls=%async_computation | async-start | bytes 4194304 | tf_op jit(solution)/shard_map/all_to_all | solution.py:80
  415.9 8.3 %copy-start.1 = (bf16[4096,22]{0,1:T(8,128)(2,1)S(1)}, bf16[4096,22]{0,1:T(8,128)(2,1)}, u32[]{:S(2)}) copy-start(bf16[4096,22]{0,1:T(8,128)(2,1)} %param.7) | copy-start | bytes 540676
Sparse Core Ops, SparseCore 0:
  8.9 203.7 all-gather.1
where the time goes:
time: 431 us
  waiting for transfers between devices  249 us (58%)
  other arithmetic  74.5 us (17%)
  matrix products  52.9 us (12%)
  local copies, waits for them, and re-layouts  37.8 us (9%)
  between operations  13.5 us (3%)
    all_gather x1, waiting for transfers between devices, local(): whole_basis = lax.all_gather(mode_basis, 'wave', axis=1, tiled=True)  200 us
    another operation x2, other arithmetic  68.4 us
    all_to_all x1, waiting for transfers between devices, local(): lax.all_to_all(spectra, 'wave', split_axis=2, concat_axis=1, tiled=True)  47.6 us
    dot_general x1, matrix products, local(): jnp.dot(coeffs, whole_basis.reshape(mode_count, -1), preferred_element_ty...  24.2 us
    dot_general x1, matrix products, pupil_section(): jnp.einsum('flxy,luy->flxu', pupil_field, kernel_table, preferred_element...  14.6 us
    dot_general x1, matrix products, finish_section(): jnp.einsum('lux,flxv->fluv', kernel_table, stacked, preferred_element_typ...  11 us
    another operation x1, local copies, waits for them, and re-layouts  9.99 us
  transfers between devices with their start and end apart: 2, of which 2 were waited for; matrix products, arithmetic and copies ran while one was open for 1% of the time, Pallas kernels for 0%

commit v1 on v0

--- a/solution.py
+++ b/solution.py
@@ -77,7 +77,10 @@
     path_diff = path_diff.reshape(positions, PUP, PUP)
     first_pass = pupil_section(path_diff, wave_lengths, kernel_table, 0)
     spectra = finish_section(first_pass, kernel_table)
-    pixel_slabs = lax.all_to_all(spectra, "wave", split_axis=2, concat_axis=1, tiled=True)
+    pixel_slabs = jnp.concatenate(
+        lax.all_to_all(jnp.stack(jnp.split(spectra, lax.axis_size("wave"), axis=2)), "wave", 0, 0),
+        axis=1,
+    )
     sed_rows = sed_table.shape[0]
     one_hot = (
         template_ids[:, :, None] == jnp.arange(sed_rows, dtype=jnp.int32)[None, None, :]

time: 431 us -> 437 us (1.014)
    reshape x0 -> x2, local copies, waits for them, and re-layouts: none -> 6.26 us  [local(): jnp.concatenate(lax.all_to_all(jnp.stack(jnp.split(spectra, lax.axis_size...]
    another operation x1 -> x3, local copies, waits for them, and re-layouts: 9.99 us -> 15.9 us
    all_to_all x2 -> x0, local copies, waits for them, and re-layouts: 5.72 us -> none  [local(): lax.all_to_all(spectra, 'wave', split_axis=2, concat_axis=1, tiled=True)]
    another operation x2 -> x3, other arithmetic: 68.4 us -> 70.9 us
where the time goes in v1:
time: 437 us
  waiting for transfers between devices  249 us (57%)
  other arithmetic  77 us (18%)
  matrix products  52.9 us (12%)
  local copies, waits for them, and re-layouts  41.3 us (9%)
  between operations  13.5 us (3%)
    all_gather x1, waiting for transfers between devices, local(): whole_basis = lax.all_gather(mode_basis, 'wave', axis=1, tiled=True)  200 us
    another operation x2, other arithmetic  68.4 us
    all_to_all x1, waiting for transfers between devices, local(): lax.all_to_all(jnp.stack(jnp.split(spectra, lax.axis_size('wave'), axis=2...  47.6 us
    dot_general x1, matrix products, local(): jnp.dot(coeffs, whole_basis.reshape(mode_count, -1), preferred_element_ty...  24.2 us
    dot_general x1, matrix products, pupil_section(): jnp.einsum('flxy,luy->flxu', pupil_field, kernel_table, preferred_element...  14.6 us
    dot_general x1, matrix products, finish_section(): jnp.einsum('lux,flxv->fluv', kernel_table, stacked, preferred_element_typ...  11 us
    another operation x1, local copies, waits for them, and re-layouts  9.99 us
  transfers between devices with their start and end apart: 2, of which 2 were waited for; matrix products, arithmetic and copies ran while one was open for 1% of the time, Pallas kernels for 0%

profile of v1, /device:TPU:0, one launch (start us, length us, event | category | flops | bytes accessed | tf_op | source)
XLA Modules:
  0.0 436.9 jit_solution(1968816101486275504)
XLA Ops:
  6.5 0.0 copy-start
  6.5 0.0 all-gather.2.cloned.1.call-start
  6.5 0.7 all-gather.2.cloned.1.call-update
  7.3 0.7 broadcast_divide_fusion.1
  8.0 0.1 multiply_convert_fusion
  8.1 0.2 fusion.30
  8.3 4.1 fusion.22
  12.4 0.0 copy-start.3
  12.4 200.3 %all-gather.2.cloned.1.call-done = bf16[22,512,512]{2,1,0:T(8,128)(2,1)} async-done(((bf16[22,128,512]{2,1,0:T(8,128)(2,1)}), bf16[22,512,512]{2,1,0:T(8,128)(2,1)}) %all-gather.2.cloned.1.call-update) | async-done | bytes 11534352 | tf_op jit(solution)/shard_map/all_gather | solution.py:73
  212.7 10.0 %slice_bitcast_fusion = bf16[512,512,22]{1,0,2:T(8,128)(2,1)} fusion(bf16[22,512,512]{2,1,0:T(8,128)(2,1)} %all-gather.2.cloned.1.call-done), kind=kLoop, calls=%fused_computation.13 | loop fusion | bytes 23068672 | tf_op jit(solution)/shard_map/reshape.41
  222.7 0.0 copy-done
  222.7 0.0 copy-done.3
  222.7 24.2 %fusion.9 = f32[8,512,512]{2,0,1:T(8,128)} fusion(bf16[512,512,22]{1,0,2:T(8,128)(2,1)} %slice_bitcast_fusion, bf16[4096,22]{0,1:T(8,128)(2,1)S(1)} %copy-done, s32[8]{0:T(128)S(1)} %copy-done.3), kind=kOutput, calls=%fused_computation.11 | convolution fusion | flops 93749424 | bytes 20103200 | tf_op jit(solution)/shard_map/dot_general | solution.py:74
  246.9 8.2 %copy.19 = f32[8,512,512]{2,1,0:T(8,128)S(1)} copy(f32[8,512,512]{2,0,1:T(8,128)} %fusion.9) | data formatting | bytes 16777216 | tf_op jit(solution)/shard_map/dot_general | solution.py:74
  255.2 64.3 %fusion.2 = (bf16[8,2,512,512]{3,2,0,1:T(8,128)(2,1)}, bf16[8,2,512,512]{3,2,0,1:T(8,128)(2,1)}) fusion(f32[2]{0:T(128)S(1)} %get-tuple-element.17, f32[8,512,512]{2,1,0:T(8,128)S(1)} %copy.19, f32[512,512]{1,0:T(8,128)S(1)} %fusion.30), kind=kLoop, calls=%fused_computation.4 | loop fusion | flops 20971520 | bytes 26214408 | tf_op jit(solution)/shard_map/convert
  319.5 14.6 %convert_bitcast_fusion = bf16[8,2,512,512]{3,2,0,1:T(8,128)(2,1)} fusion(bf16[8,2,512,512]{3,2,0,1:T(8,128)(2,1)} %get-tuple-element.6, bf16[8,2,512,512]{3,2,0,1:T(8,128)(2,1)} %get-tuple-element.5, bf16[2,256,512]{2,1,0:T(8,128)(2,1)S(1)} %get-tuple-element.15, bf16[2,256,512]{2,1,0:T(8,128)(2,1)S(1)} %get-tuple-element.14, ...), kind=kOutput, calls=%fused_computation.18 | convolution fusion | flops 8636071936 | bytes 26738688 | tf_op jit(solution)/shard_map/flxy,luy->flxu/dot_general | solution.py:44
  334.1 5.8 %fusion.41 = (bf16[8,2,512,256]{3,2,0,1:T(8,128)(2,1)}, bf16[8,2,512,256]{3,2,0,1:T(8,128)(2,1)}) fusion(bf16[8,2,512,512]{3,2,0,1:T(8,128)(2,1)} %convert_bitcast_fusion), kind=kLoop, calls=%fused_computation.63 | loop fusion | bytes 16777216 | tf_op jit(solution)/shard_map/slice | solution.py:52
  339.9 11.0 %fusion.18 = f32[8,2,512,256]{2,3,0,1:T(8,128)} fusion(bf16[8,2,512,256]{3,2,0,1:T(8,128)(2,1)} %get-tuple-element.8, bf16[8,2,512,256]{3,2,0,1:T(8,128)(2,1)} %get-tuple-element.7, bf16[2,256,512]{2,1,0:T(8,128)(2,1)S(1)} %get-tuple-element.15, bf16[2,256,512]{2,1,0:T(8,128)(2,1)S(1)} %get-tuple-element.14, bf16[2,256,512]{2,1,0:T(8,128)(2,1)S(1)} %get-tuple-element.13), kind=kOutput, calls=%fused_computation.24 | convolution fusion | flops 4320133120 | bytes 18350080 | tf_op jit(solution)/shard_map/lux,flxv->fluv/dot_general | solution.py:53
  350.9 4.3 fusion.31
  355.2 1.6 copy-done.2
  356.8 0.8 divide_convert_fusion
  357.6 1.2 slice_bitcast_fusion.4
  358.7 2.5 pad_maximum_fusion
  361.3 4.8 %copy.21 = bf16[4,8,2,64,256]{4,3,2,1,0:T(8,128)(2,1)} copy(bf16[4,8,2,64,256]{3,4,1,2,0:T(8,128)(2,1)} %pad_maximum_fusion) | data formatting | bytes 4194304 | tf_op jit(solution)/shard_map/stack | solution.py:81
  366.0 3.6 all-to-all-start
  369.6 0.0 copy-done.4
  369.7 1.0 fusion.32
  370.7 47.6 %all-to-all-done = bf16[4,8,2,64,256]{4,3,2,1,0:T(8,128)(2,1)S(1)} async-done(((bf16[4,8,2,64,256]{4,3,2,1,0:T(8,128)(2,1)}), bf16[4,8,2,64,256]{4,3,2,1,0:T(8,128)(2,1)S(1)}, u32[]{:S(2)}, u32[]{:S(2)}) %all-to-all-start) | async-done | bytes 2097184 | tf_op jit(solution)/shard_map/all_to_all | solution.py:81
  418.3 3.5 copy.22
  421.8 2.8 reshape.109
  424.6 2.0 convolution_convert_fusion
  426.6 3.5 copy.24
  (10 shorter events, 0.0 us)
Async XLA Ops:
  6.5 216.2 %copy-start = (bf16[4096,22]{0,1:T(8,128)(2,1)S(1)}, bf16[4096,22]{0,1:T(8,128)(2,1)}, u32[]{:S(2)}) copy-start(bf16[4096,22]{0,1:T(8,128)(2,1)} %param.7) | copy-start | bytes 540676
  6.5 206.2 %all-gather.2.cloned.1.call-start = ((), (), s32[]{:S(2)}) async-start(), calls=%async_computation.1 | async-start | bytes 14417920 | tf_op jit(solution)/shard_map/all_gather | solution.py:73
  12.4 210.3 %copy-start.3 = (s32[8]{0:T(128)S(1)}, s32[8]{0:T(128)}, u32[]{:S(2)}) copy-start(s32[8]{0:T(128)} %param.8) | copy-start | bytes 100
  350.9 5.8 %copy-start.2 = (f32[8,2,512,256]{2,3,0,1:T(8,128)S(1)}, f32[8,2,512,256]{2,3,0,1:T(8,128)}, u32[]{:S(2)}) copy-start(f32[8,2,512,256]{2,3,0,1:T(8,128)} %fusion.18) | copy-start | bytes 25165828
  361.2 8.4 %copy-start.4 = (f32[1024,8]{0,1:T(8,128)S(1)}, f32[1024,8]{0,1:T(8,128)}, u32[]{:S(2)}) copy-start(f32[1024,8]{0,1:T(8,128)} %param.10) | copy-start | bytes 98308
  361.3 8.4 %copy-start.5 = (s32[8,8]{1,0:T(8,128)S(1)}, s32[8,8]{1,0:T(8,128)}, u32[]{:S(2)}) copy-start(s32[8,8]{1,0:T(8,128)} %param.11) | copy-start | bytes 772
  366.0 52.3 %all-to-all-start = ((bf16[4,8,2,64,256]{4,3,2,1,0:T(8,128)(2,1)}), bf16[4,8,2,64,256]{4,3,2,1,0:T(8,128)(2,1)S(1)}, u32[]{:S(2)}, u32[]{:S(2)}) async-start(bf16[4,8,2,64,256]{4,3,2,1,0:T(8,128)(2,1)} %copy.21), calls=%async_computation | async-start | bytes 4194304 | tf_op jit(solution)/shard_map/all_to_all | solution.py:81
  421.8 8.3 %copy-start.1 = (bf16[4096,22]{0,1:T(8,128)(2,1)S(1)}, bf16[4096,22]{0,1:T(8,128)(2,1)}, u32[]{:S(2)}) copy-start(bf16[4096,22]{0,1:T(8,128)(2,1)} %param.7) | copy-start | bytes 540676
Sparse Core Ops, SparseCore 0:
  8.9 203.7 all-gather.1
